TPU v7x, 512 devices: a whole 4x8x8 slice. The times are simulated.
512 devices in a mesh: seq: 32 (over z, x), dp: 2 (over core), tensor: 8 (over y).
Axes of the slice: x: 4, y: 8, z: 8, core: 2. Of those that a mesh axis runs over, the one named last changes fastest.
Arguments:
- head_inputs: bfloat16 [2, 2560, 16384], P('dp', 'tensor', 'seq'), may hold values from -6 to 6
- b_proj: bfloat16 [2, 16384, 128], P('dp', 'seq'), may hold values from -0.59765625 to 0.59765625
- c_proj: bfloat16 [2, 16384, 128], P('dp', 'seq'), may hold values from -0.59765625 to 0.59765625
- dt_raw: float32 [2, 40, 16384], P('dp', 'tensor', 'seq'), may hold values from -2 to 0
- a_log: float32 [40], P('tensor'), as said below
- d_skip: float32 [40], P('tensor'), may hold values from 0.5 to 1.5
- w_out: bfloat16 [2560, 2560], P('tensor', 'dp'), may hold values from -0.125 to 0.125
- out_grad: bfloat16 [2, 2560, 16384], P('dp', 'tensor', 'seq'), may hold values from -6 to 6
Outputs:
- mixed: bfloat16 [2, 2560, 16384], P('dp', 'tensor', 'seq')
- grad_inputs: bfloat16 [2, 2560, 16384], P('dp', 'tensor', 'seq')
- grad_b: bfloat16 [2, 16384, 128], P('dp', 'seq')
- grad_c: bfloat16 [2, 16384, 128], P('dp', 'seq')
- grad_dt: float32 [2, 40, 16384], P('dp', 'tensor', 'seq')
- grad_alog: float32 [40], P('tensor')
- grad_skip: float32 [40], P('tensor')
- grad_w: bfloat16 [2560, 2560], P('tensor', ('seq', 'dp'))
Inputs may be any that keep to these rules, and one draw needn't show every extreme that they name: exp(a_log) lies between 0.1 / 16384 and 0.1.
All inputs are finite; a program needn't handle non-finite values.
Results may differ from a plain program's by a relative error of at most 0.0049.
Values may be sent and summed in bfloat16 or wider, within the bound.
A program may use at most 128 MiB of HBM per device.

v0:
```python
import jax
import jax.numpy as jnp
from jax import lax
from jax.sharding import PartitionSpec as P

SPAN = 256
HIGH = lax.Precision.HIGHEST


def span_pass(carried, x_block, b_block, c_block, step_block, decay_rate):
    log_decay = step_block * decay_rate[:, None]
    cumulative = jnp.cumsum(log_decay, axis=1)
    block = cumulative.shape[1]
    indices = jnp.arange(block)
    causal = (indices[:, None] >= indices[None, :])[None, :, :]
    spread = cumulative[:, :, None] - cumulative[:, None, :]
    weights = jnp.where(causal, jnp.exp(jnp.where(causal, spread, 0.0)), 0.0)
    affinity = jnp.dot(c_block, b_block.T, precision=HIGH)
    scores = affinity[None, :, :] * weights * step_block[:, None, :]
    block_out = jnp.einsum("hps,hts->hpt", x_block, scores, precision=HIGH)
    block_out = block_out + jnp.exp(cumulative)[:, None, :] * jnp.einsum(
        "hpn,tn->hpt", carried, c_block, precision=HIGH
    )
    tail_weight = jnp.exp(cumulative[:, -1:] - cumulative) * step_block
    updated = jnp.exp(cumulative[:, -1])[:, None, None] * carried
    updated = updated + jnp.einsum(
        "hps,sn->hpn", x_block * tail_weight[:, None, :], b_block, precision=HIGH
    )
    return (updated, block_out)


def sweep(streams, b_rows, c_rows, dt_rows, alog_part, skip_part, state_in):
    head_count, head_width, length = streams.shape
    blocks = length // SPAN
    step_size = jax.nn.softplus(dt_rows)
    decay_rate = -jnp.exp(alog_part)
    x_blocks = streams.reshape(head_count, head_width, blocks, SPAN).transpose(2, 0, 1, 3)
    b_blocks = b_rows.reshape(blocks, SPAN, b_rows.shape[1])
    c_blocks = c_rows.reshape(blocks, SPAN, c_rows.shape[1])
    s_blocks = step_size.reshape(head_count, blocks, SPAN).transpose(1, 0, 2)

    def advance(carried, inputs):
        return span_pass(carried, inputs[0], inputs[1], inputs[2], inputs[3], decay_rate)

    state_end, outputs = lax.scan(advance, state_in, (x_blocks, b_blocks, c_blocks, s_blocks))
    mixed_f = outputs.transpose(1, 2, 0, 3).reshape(head_count, head_width, length)
    return (mixed_f + skip_part[:, None, None] * streams, state_end)


def per_device(head_inputs, b_proj, c_proj, dt_raw, a_log, d_skip, w_out, out_grad):
    head_count = dt_raw.shape[1]
    length = head_inputs.shape[2]
    head_width = head_inputs.shape[1] // head_count
    streams = head_inputs[0].astype(jnp.float32).reshape(head_count, head_width, length)
    b_rows = b_proj[0].astype(jnp.float32)
    c_rows = c_proj[0].astype(jnp.float32)
    dt_rows = dt_raw[0]
    decay_rate = -jnp.exp(a_log)
    step_size = jax.nn.softplus(dt_rows)
    cumulative = jnp.cumsum(step_size * decay_rate[:, None], axis=1)
    device_decay = cumulative[:, -1]
    tail_weight = jnp.exp(device_decay[:, None] - cumulative) * step_size
    local_state = jnp.einsum(
        "hpt,tn->hpn", streams * tail_weight[:, None, :], b_rows, precision=HIGH
    )
    totals = lax.all_gather(device_decay[None, :], "seq", axis=0, tiled=True)
    prefix = jnp.cumsum(totals, axis=0)
    my_index = lax.axis_index("seq")
    reached = lax.dynamic_index_in_dim(prefix, my_index, 0, keepdims=False)
    before = reached - device_decay
    shard_part = lax.all_gather(local_state[None], "seq", axis=0, tiled=True)
    row_count = shard_part.shape[0]
    indices = jnp.arange(row_count, dtype=jnp.int32)
    prefix_ends = prefix
    active = (indices < my_index)[:, None]
    weights = jnp.where(active, jnp.exp(jnp.where(active, before[None, :] - prefix_ends, 0.0)), 0.0)
    state_in = jnp.einsum("jh,jhpn->hpn", weights, shard_part, precision=HIGH)

    def local_sweep(xa, ba, ca, da, aa, sa):
        return sweep(xa, ba, ca, da, aa, sa, state_in)

    primal, pullback = jax.vjp(local_sweep, streams, b_rows, c_rows, dt_rows, a_log, d_skip)
    mixed_half = primal[0].reshape(head_count * head_width, length).astype(jnp.bfloat16)
    g_full = lax.all_gather(out_grad[0], "tensor", axis=0, tiled=True)
    cotan_sum = jnp.dot(
        lax.all_gather(w_out, "dp", axis=1, tiled=True), g_full, preferred_element_type=jnp.float32
    )
    cotan_half = cotan_sum.astype(jnp.bfloat16)
    y_cotan = (
        lax.optimization_barrier(cotan_half)
        .astype(jnp.float32)
        .reshape(head_count, head_width, length)
    )
    local_cotan = jnp.einsum(
        "hpt,tn->hpn", y_cotan * jnp.exp(cumulative)[:, None, :], c_rows, precision=HIGH
    )
    shard_part = lax.all_gather(local_cotan[None], "seq", axis=0, tiled=True)
    row_count = shard_part.shape[0]
    indices = jnp.arange(row_count, dtype=jnp.int32)
    prefix_ends = prefix
    active = (indices > my_index)[:, None]
    weights = jnp.where(
        active, jnp.exp(jnp.where(active, prefix_ends - totals - reached[None, :], 0.0)), 0.0
    )
    cotan_in = jnp.einsum("jh,jhpn->hpn", weights, shard_part, precision=HIGH)
    grads = pullback((y_cotan, cotan_in))
    w_terms = lax.dot_general(
        mixed_half, g_full, (((1,), (1,)), ((), ())), preferred_element_type=jnp.float32
    )
    grad_w = lax.psum_scatter(w_terms, ("seq", "dp"), scatter_dimension=1, tiled=True).astype(
        jnp.bfloat16
    )
    grad_b, grad_c = lax.psum((grads[1], grads[2]), "tensor")
    grad_alog, grad_skip = lax.psum((grads[4], grads[5]), ("seq", "dp"))
    grad_inputs = grads[0].reshape(head_count * head_width, length).astype(jnp.bfloat16)
    return (
        mixed_half[None],
        grad_inputs[None],
        grad_b.astype(jnp.bfloat16)[None],
        grad_c.astype(jnp.bfloat16)[None],
        grads[3][None],
        grad_alog,
        grad_skip,
        grad_w,
    )


def solution(mesh):
    in_specs = (
        P("dp", "tensor", "seq"),
        P("dp", "seq", None),
        P("dp", "seq", None),
        P("dp", "tensor", "seq"),
        P("tensor"),
        P("tensor"),
        P("tensor", "dp"),
        P("dp", "tensor", "seq"),
    )
    out_specs = (
        P("dp", "tensor", "seq"),
        P("dp", "tensor", "seq"),
        P("dp", "seq", None),
        P("dp", "seq", None),
        P("dp", "tensor", "seq"),
        P("tensor"),
        P("tensor"),
        P("tensor", ("seq", "dp")),
    )
    return jax.shard_map(
        per_device, mesh=mesh, in_specs=in_specs, out_specs=out_specs, check_vma=False
    )
```

profile of v0, /device:TPU:16, one launch (start us, length us, event | category | flops | bytes accessed | tf_op | source)
XLA Modules:
  0.0 658.8 jit_solution(519363650831749236)
XLA Ops:
  10.1 1.5 reduce-window.46
  15.4 17.3 %all-gather.9.cloned.1.call-done = bf16[320,2560]{1,0:T(8,128)(2,1)} async-done(((bf16[320,1280]{1,0:T(8,128)(2,1)}), bf16[320,2560]{1,0:T(8,128)(2,1)}) %all-gather.9.cloned.1.call-update) | async-done | bytes 1638416 | tf_op jit(solution)/shard_map/all_gather | solution.py:86
  32.7 47.4 %all-gather.13.cloned.1.call-done = bf16[1,2560,512]{2,1,0:T(8,128)(2,1)} async-done(((bf16[1,320,512]{2,1,0:T(8,128)(2,1)}), bf16[1,2560,512]{2,1,0:T(8,128)(2,1)}) %all-gather.13.cloned.1.call-update) | async-done | bytes 2621456 | tf_op jit(solution)/shard_map/all_gather | solution.py:84
  80.0 3.2 fusion.131
  87.3 76.9 %all-reduce.2 = f32[160]{0:T(256)S(1)} all-reduce(f32[160]{0:T(256)S(1)} %dynamic-update-slice), channel_id=2, replica_groups=mesh['seq'=32,'dp'=2,'tensor'=8] {'seq'}, use_global_device_ids=true, to_apply=%add.2 | all-reduce | flops 160 | bytes 1280
  167.5 7.2 %all-gather.11.cloned.1.call-done = f32[160,64,128]{2,1,0:T(8,128)} async-done(((f32[5,64,128]{2,1,0:T(8,128)}), f32[160,64,128]{2,1,0:T(8,128)}) %all-gather.11.cloned.1.call-update) | async-done | bytes 5242896 | tf_op jit(solution)/shard_map/all_gather | solution.py:71
  174.6 7.7 %fusion.125 = f32[5,1,64,128]{3,1,2,0:T(1,128)S(1)} fusion(f32[32,5,1,1]{0,2,3,1:T(1,128)S(1)} %copy.117, f32[32,5,64,128]{3,2,1,0:T(8,128)} %bitcast.487), kind=kOutput, calls=%fused_computation.159 | convolution fusion | flops 15728640 | bytes 5407360 | tf_op jit(solution)/shard_map/jh,jhpn->hpn/dot_general | solution.py:77
  185.1 23.1 %while.75 = (s32[]{:T(128)}, f32[5,64,128]{2,1,0:T(8,128)S(1)}, f32[2,5,64,256]{3,2,1,0:T(8,128)}, f32[2,5,256,256]{3,2,1,0:T(8,128)}, f32[2,128,256]{1,2,0:T(8,...) while((s32[]{:T(128)}, f32[5,64,128]{2,1,0:T(8,128)S(1)}, ...), condition=%wide.region_6.7_spmd.clone.clone, body=%wide.region_3.6_spmd.clone.clone.sunk | while | flops 607838976 | bytes 16159797 | solution.py:45
  185.2 1.5 reduce-window.60
  188.2 2.8 multiply_dynamic-update-slice_fusion.4
  192.4 2.4 fusion.212
  196.8 1.5 reduce-window.60
  199.8 2.8 multiply_dynamic-update-slice_fusion.4
  204.0 2.4 fusion.212
  208.2 1.6 copy.110
  211.3 5.4 fusion.127
  217.6 48.0 %all-gather.15.cloned.1.call-done = f32[160,64,128]{2,1,0:T(8,128)} async-done(((f32[5,64,128]{2,1,0:T(8,128)}), f32[160,64,128]{2,1,0:T(8,128)}) %all-gather.15.cloned.1.call-update) | async-done | bytes 5242896 | tf_op jit(solution)/shard_map/all_gather | solution.py:97
  265.6 7.7 %fusion.123 = f32[5,1,64,128]{3,1,2,0:T(1,128)S(1)} fusion(f32[32,5,1,1]{0,2,3,1:T(1,128)S(1)} %copy.120, f32[32,5,64,128]{3,2,1,0:T(8,128)} %bitcast.486), kind=kOutput, calls=%fused_computation.157 | convolution fusion | flops 15728640 | bytes 5407360 | tf_op jit(solution)/shard_map/jh,jhpn->hpn/dot_general | solution.py:105
  275.7 46.3 %while.76 = (s32[]{:T(128)}, f32[5]{0:T(128)S(1)}, f32[5,64,128]{2,1,0:T(8,128)S(1)}, f32[2,5,64,256]{3,2,1,0:T(8,128)}, f32[2,256,128]{2,1,0:T(8,128)}, /*index...) while((s32[]{:T(128)}, f32[5]{0:T(128)S(1)}, ...), condition=%wide.region_19.20_spmd.clone.clone, body=%wide.region_7.19_spmd.clone.clone.sunk | while | flops 1212566272 | bytes 13529267 | solution.py:45
  276.7 3.9 fusion.227
  282.7 6.3 reduce-window.62
  290.2 1.9 fusion.240
  292.4 1.8 convolution_bitcast_fusion.5
  295.4 3.0 fusion.238
  299.9 3.9 fusion.227
  305.9 6.3 reduce-window.62
  313.4 1.9 fusion.240
  315.5 1.8 convolution_bitcast_fusion.5
  318.6 3.0 fusion.238
  322.1 1.6 copy.114
  325.6 290.5 %all-reduce.8 = (f32[5]{0:T(128)}, f32[5]{0:T(128)}, bf16[320,2560]{0,1:T(8,128)(2,1)S(1)}) all-reduce(f32[5]{0:T(128)S(1)} %negate_multiply_fusion, f32[5]{0:T(128)S(1)} %reduce_sum.212, f32[320,2560]{0,1:T(8,128)} %fusion.127), channel_id=1, replica_groups=mesh['seq'=32,'dp'=2,'tensor'=8] {'seq','dp'}, use_global_device_ids=true, to_apply=%region_22.23 | all-reduce | flops 819210 | bytes 4915280 | tf_op jit(solution)/shard_map/psum | solution.py:114
  616.8 35.5 %all-reduce.9 = (bf16[512,128]{1,0:T(8,128)(2,1)}, bf16[512,128]{1,0:T(8,128)(2,1)}) all-reduce(f32[512,128]{1,0:T(8,128)S(1)} %bitcast.502, f32[512,128]{1,0:T(8,128)S(1)} %bitcast.503), channel_id=1, replica_groups=mesh['seq'=32,'dp'=2,'tensor'=8] {'tensor'}, use_global_device_ids=true, to_apply=%region_20.21 | all-reduce | flops 131072 | bytes 786432 | tf_op jit(solution)/shard_map/psum | solution.py:113
  (224 shorter events, 44.2 us)
Async XLA Ops:
  7.2 7.0 %copy-start.8 = (bf16[1,512,128]{2,1,0:T(8,128)(2,1)S(1)}, bf16[1,512,128]{2,1,0:T(8,128)(2,1)}, u32[]{:S(2)}) copy-start(bf16[1,512,128]{2,1,0:T(8,128)(2,1)} %param.13) | copy-start | bytes 393220
  7.2 25.5 %all-gather.9.cloned.1.call-start = ((), (), s32[]{:S(2)}) async-start(), calls=%async_computation | async-start | bytes 2457600 | tf_op jit(solution)/shard_map/all_gather | solution.py:86
  7.9 72.1 %all-gather.13.cloned.1.call-start = ((), (), s32[]{:S(2)}) async-start(), calls=%async_computation.2 | async-start | bytes 2949120 | tf_op jit(solution)/shard_map/all_gather | solution.py:84
  8.7 166.0 %all-gather.11.cloned.1.call-start = ((), (), s32[]{:S(2)}) async-start(), calls=%async_computation.1 | async-start | bytes 5406720 | tf_op jit(solution)/shard_map/all_gather | solution.py:71
  15.3 68.1 %copy-start.9 = (bf16[1,512,128]{2,1,0:T(8,128)(2,1)S(1)}, bf16[1,512,128]{2,1,0:T(8,128)(2,1)}, u32[]{:S(2)}) copy-start(bf16[1,512,128]{2,1,0:T(8,128)(2,1)} %param.14) | copy-start | bytes 393220
  15.3 69.2 %copy-start = (bf16[1,320,512]{2,1,0:T(8,128)(2,1)S(1)}, bf16[1,320,512]{2,1,0:T(8,128)(2,1)}, u32[]{:S(2)}) copy-start(bf16[1,320,512]{2,1,0:T(8,128)(2,1)} %param.12) | copy-start | bytes 983044
  15.3 250.2 %all-gather.15.cloned.1.call-start = ((), (), s32[]{:S(2)}) async-start(), calls=%async_computation.3 | async-start | bytes 5406720 | tf_op jit(solution)/shard_map/all_gather | solution.py:97
  83.3 83.7 %copy-start.3 = (bf16[320,512]{1,0:T(8,128)(2,1)}, bf16[320,512]{1,0:T(8,128)(2,1)S(1)}, u32[]{:S(2)}) copy-start(bf16[320,512]{1,0:T(8,128)(2,1)S(1)} %fusion.131) | copy-start | bytes 983044
  83.3 81.4 %copy-start.10 = (f32[1,5,512]{2,0,1:T(1,128)S(1)}, f32[1,5,512]{2,0,1:T(1,128)}, u32[]{:S(2)}) copy-start(f32[1,5,512]{2,0,1:T(1,128)} %param.15) | copy-start | bytes 30724
  83.3 81.6 %copy-start.11 = (f32[5]{0:T(128)S(1)}, f32[5]{0:T(128)}, u32[]{:S(2)}) copy-start(f32[5]{0:T(128)} %param.17) | copy-start | bytes 64
  191.2 3.7 copy-start.1
  194.9 0.8 copy-start.2
  202.8 3.6 copy-start.1
  206.4 0.8 copy-start.2
  211.3 5.4 copy-start.5
  322.0 1.7 copy-start.4
  322.0 2.7 copy-start.12
  323.8 293.0 %copy-start.6 = (f32[2,256,128]{2,1,0:T(8,128)S(1)}, f32[2,256,128]{2,1,0:T(8,128)}, u32[]{:S(2)}) copy-start(f32[2,256,128]{2,1,0:T(8,128)} %get-tuple-element.972) | copy-start | bytes 786436
  323.8 293.0 %copy-start.7 = (f32[2,256,128]{2,1,0:T(8,128)S(1)}, f32[2,256,128]{2,1,0:T(8,128)}, u32[]{:S(2)}) copy-start(f32[2,256,128]{2,1,0:T(8,128)} %get-tuple-element.973) | copy-start | bytes 786436
Sparse Core Ops, SparseCore 0:
  10.1 22.5 all-gather.8
  34.7 45.2 all-gather.12
  83.8 90.8 all-gather.10
  177.7 87.8 all-gather.14
where the time goes:
time: 660 us; the launch traced here: 659 us
  blocking collectives  403 us (61%)
  waiting for transfers between devices  121 us (18%)
  matrix products  63.7 us (10%)
  other arithmetic  33.6 us (5%)
  local copies, waits for them, and re-layouts  21.4 us (3%)
  between operations  15.6 us (2%)
    psum x1, blocking collectives, per_device(): grad_alog, grad_skip = lax.psum((grads[4], grads[5]), ('seq', 'dp'))  291 us
    unnamed x1, blocking collectives  76.9 us
    all_gather x1, waiting for transfers between devices, per_device(): shard_part = lax.all_gather(local_cotan[None], 'seq', axis=0, tiled=True)  48 us
    all_gather x1, waiting for transfers between devices, per_device(): g_full = lax.all_gather(out_grad[0], 'tensor', axis=0, tiled=True)  47.4 us
    psum x1, blocking collectives, per_device(): grad_b, grad_c = lax.psum((grads[1], grads[2]), 'tensor')  35.5 us
    dot_general x6, matrix products, span_pass(): block_out = jnp.einsum('hps,hts->hpt', x_block, scores, precision=HIGH)  18.5 us
    another operation x23, other arithmetic  17.6 us
    all_gather x1, waiting for transfers between devices, per_device(): lax.all_gather(w_out, 'dp', axis=1, tiled=True)  17.3 us
  transfers between devices with their start and end apart: 4, of which 4 were waited for; matrix products, arithmetic and copies ran while one was open for 9% of the time, Pallas kernels for 0%

commit v1 on v0

--- a/solution.py
+++ b/solution.py
@@ -81,7 +81,23 @@
 
     primal, pullback = jax.vjp(local_sweep, streams, b_rows, c_rows, dt_rows, a_log, d_skip)
     mixed_half = primal[0].reshape(head_count * head_width, length).astype(jnp.bfloat16)
-    g_full = lax.all_gather(out_grad[0], "tensor", axis=0, tiled=True)
+    ways, here, step = (lax.axis_size("tensor"), lax.axis_index("tensor"), out_grad[0].shape[0])
+    dims = [n * ways if d == 0 else n for d, n in enumerate(out_grad[0].shape)]
+    full = lax.dynamic_update_slice_in_dim(
+        jnp.zeros(dims, out_grad[0].dtype), out_grad[0], here * step, axis=0
+    )
+    going_up = going_down = out_grad[0]
+    for far in range(1, ways // 2 + 1):
+        going_up = lax.ppermute(going_up, "tensor", [(d, (d + 1) % ways) for d in range(ways)])
+        full = lax.dynamic_update_slice_in_dim(full, going_up, (here - far) % ways * step, axis=0)
+        if 2 * far < ways:
+            going_down = lax.ppermute(
+                going_down, "tensor", [(d, (d - 1) % ways) for d in range(ways)]
+            )
+            full = lax.dynamic_update_slice_in_dim(
+                full, going_down, (here + far) % ways * step, axis=0
+            )
+    g_full = full
     cotan_sum = jnp.dot(
         lax.all_gather(w_out, "dp", axis=1, tiled=True), g_full, preferred_element_type=jnp.float32
     )

time: 660 us -> 613 us (0.929)
  waiting for transfers between devices: 121 us -> 37.8 us
  starting transfers between devices: 0.16 us -> 24 us
  local copies, waits for them, and re-layouts: 21.4 us -> 32.9 us
    all_gather x1 -> x0, waiting for transfers between devices: 47.4 us -> none  [per_device(): g_full = lax.all_gather(out_grad[0], 'tensor', axis=0, tiled=True)]
    all_gather x1, waiting for transfers between devices: 48 us -> 22.1 us  [per_device(): shard_part = lax.all_gather(local_cotan[None], 'seq', axis=0, tiled=True)]
    ppermute x0 -> x7, starting transfers between devices: none -> 23.9 us  [the longest x4 17.7 us: per_device(): lax.ppermute(going_up, 'tensor', [(d, (d + 1) % ways) for d in range(ways)])]
    all_gather x1, waiting for transfers between devices: 17.3 us -> 0.02 us  [per_device(): lax.all_gather(w_out, 'dp', axis=1, tiled=True)]
    ppermute x0 -> x7, waiting for transfers between devices: none -> 15 us  [the longest x4 12.7 us: per_device(): lax.ppermute(going_up, 'tensor', [(d, (d + 1) % ways) for d in range(ways)])]
    all_gather x1, waiting for transfers between devices: 7.17 us -> 0.02 us  [per_device(): shard_part = lax.all_gather(local_state[None], 'seq', axis=0, tiled=True)]
  transfers between devices with their start and end apart: 4 -> 10, of which waited for: 4 -> 7; matrix products, arithmetic and copies ran while one was open for 9% -> 10% of each run, Pallas kernels for 0% -> 0%
where the time goes in v1:
time: 613 us; the launch traced here: 612 us
  blocking collectives  408 us (67%)
  matrix products  61.8 us (10%)
  waiting for transfers between devices  37.8 us (6%)
  local copies, waits for them, and re-layouts  32.9 us (5%)
  other arithmetic  31.3 us (5%)
  starting transfers between devices  24 us (4%)
  between operations  15.9 us (3%)
    psum x1, blocking collectives, per_device(): grad_alog, grad_skip = lax.psum((grads[4], grads[5]), ('seq', 'dp'))  291 us
    unnamed x1, blocking collectives  81.4 us
    psum x1, blocking collectives, per_device(): grad_b, grad_c = lax.psum((grads[1], grads[2]), 'tensor')  35.9 us
    all_gather x1, waiting for transfers between devices, per_device(): shard_part = lax.all_gather(local_cotan[None], 'seq', axis=0, tiled=True)  22.1 us
    dot_general x6, matrix products, span_pass(): block_out = jnp.einsum('hps,hts->hpt', x_block, scores, precision=HIGH)  18.7 us
    ppermute x4, starting transfers between devices, per_device(): lax.ppermute(going_up, 'tensor', [(d, (d + 1) % ways) for d in range(ways)])  17.7 us
    another operation x23, other arithmetic  17.6 us
    ppermute x4, waiting for transfers between devices, per_device(): lax.ppermute(going_up, 'tensor', [(d, (d + 1) % ways) for d in range(ways)])  12.7 us
  transfers between devices with their start and end apart: 10, of which 7 were waited for; matrix products, arithmetic and copies ran while one was open for 10% of the time, Pallas kernels for 0%

profile of v1, /device:TPU:16, one launch (start us, length us, event | category | flops | bytes accessed | tf_op | source)
XLA Modules:
  0.0 612.0 jit_solution(4444368285269199548)
XLA Ops:
  15.2 3.5 collective-permute-start
  18.7 2.4 collective-permute-start.1
  21.0 5.6 collective-permute-done
  26.6 3.7 collective-permute-start.2
  30.9 1.9 collective-permute-start.3
  33.2 4.1 collective-permute-done.2
  37.3 5.1 collective-permute-start.4
  44.4 1.9 collective-permute-start.5
  47.6 5.5 collective-permute-start.6
  55.8 1.8 collective-permute-done.6
  57.7 3.5 fusion.127
  65.3 81.4 %all-reduce.2 = f32[160]{0:T(256)S(1)} all-reduce(f32[160]{0:T(256)S(1)} %dynamic-update-slice), channel_id=2, replica_groups=mesh['seq'=32,'dp'=2,'tensor'=8] {'seq'}, use_global_device_ids=true, to_apply=%add.2 | all-reduce | flops 160 | bytes 1280
  150.0 7.8 %fusion.125 = f32[5,1,64,128]{3,1,2,0:T(1,128)S(1)} fusion(f32[32,5,1,1]{0,2,3,1:T(1,128)S(1)} %copy.117, f32[32,5,64,128]{3,2,1,0:T(8,128)} %bitcast.485), kind=kOutput, calls=%fused_computation.159 | convolution fusion | flops 15728640 | bytes 5407360 | tf_op jit(solution)/shard_map/jh,jhpn->hpn/dot_general | solution.py:77
  160.6 27.5 %while.75 = (s32[]{:T(128)}, f32[5,64,128]{2,1,0:T(8,128)S(1)}, f32[2,5,64,256]{3,2,1,0:T(8,128)}, f32[2,5,256,256]{3,2,1,0:T(8,128)}, f32[2,128,256]{1,2,0:T(8,...) while((s32[]{:T(128)}, f32[5,64,128]{2,1,0:T(8,128)S(1)}, ...), condition=%wide.region_6.7_spmd.clone.clone, body=%wide.region_3.6_spmd.clone.clone.sunk | while | flops 607838976 | bytes 37124220 | solution.py:45
  166.2 2.4 fusion.209
  168.6 2.3 multiply_dynamic-update-slice_fusion.4
  180.0 2.4 fusion.209
  182.4 2.4 multiply_dynamic-update-slice_fusion.4
  191.1 5.5 fusion.132
  197.5 22.1 %all-gather.11.cloned.1.call-done = f32[160,64,128]{2,1,0:T(8,128)} async-done(((f32[5,64,128]{2,1,0:T(8,128)}), f32[160,64,128]{2,1,0:T(8,128)}) %all-gather.11.cloned.1.call-update) | async-done | bytes 5242896 | tf_op jit(solution)/shard_map/all_gather | solution.py:113
  219.6 7.7 %fusion.123 = f32[5,1,64,128]{3,1,2,0:T(1,128)S(1)} fusion(f32[32,5,1,1]{0,2,3,1:T(1,128)S(1)} %copy.120, f32[32,5,64,128]{3,2,1,0:T(8,128)} %bitcast.486), kind=kOutput, calls=%fused_computation.157 | convolution fusion | flops 15728640 | bytes 5407360 | tf_op jit(solution)/shard_map/jh,jhpn->hpn/dot_general | solution.py:121
  229.7 45.1 %while.76 = (s32[]{:T(128)}, f32[5]{0:T(128)S(1)}, f32[5,64,128]{2,1,0:T(8,128)S(1)}, f32[2,5,64,256]{3,2,1,0:T(8,128)}, f32[2,256,128]{2,1,0:T(8,128)}, /*index...) while((s32[]{:T(128)}, f32[5]{0:T(128)S(1)}, ...), condition=%wide.region_19.20_spmd.clone.clone, body=%wide.region_7.19_spmd.clone.clone.sunk | while | flops 1212566272 | bytes 20345160 | solution.py:45
  231.4 4.0 fusion.224
  236.5 6.3 %reduce-window.62 = f32[5,2,128]{2,1,0:T(2,128)S(1)} reduce-window(f32[5,2,128]{2,1,0:T(2,128)S(1)} %reshape.769, f32[]{:T(128)} %constant.221.clone.1..sunk.1), window={size=1x1x128 pad=0_0x0_0x0_127}, to_apply=%region_14.14 | reduce-window | flops 162560 | bytes 10244 | tf_op jit(solution)/shard_map/reduce-window.20
  243.3 1.8 convolution_bitcast_fusion.5
  245.7 3.0 fusion.235
  253.9 4.0 fusion.224
  259.1 6.3 %reduce-window.62 = f32[5,2,128]{2,1,0:T(2,128)S(1)} reduce-window(f32[5,2,128]{2,1,0:T(2,128)S(1)} %reshape.769, f32[]{:T(128)} %constant.221.clone.1..sunk.1), window={size=1x1x128 pad=0_0x0_0x0_127}, to_apply=%region_14.14 | reduce-window | flops 162560 | bytes 10244 | tf_op jit(solution)/shard_map/reduce-window.20
  265.9 1.8 convolution_bitcast_fusion.5
  268.2 3.0 fusion.235
  277.6 35.9 %all-reduce.8 = (bf16[512,128]{1,0:T(8,128)(2,1)}, bf16[512,128]{1,0:T(8,128)(2,1)}) all-reduce(f32[512,128]{1,0:T(8,128)S(1)} %bitcast.501, f32[512,128]{1,0:T(8,128)S(1)} %bitcast.502), channel_id=1, replica_groups=mesh['seq'=32,'dp'=2,'tensor'=8] {'tensor'}, use_global_device_ids=true, to_apply=%region_20.21 | all-reduce | flops 131072 | bytes 786432 | tf_op jit(solution)/shard_map/psum | solution.py:129
  314.3 290.5 %all-reduce.9 = (f32[5]{0:T(128)}, f32[5]{0:T(128)}, bf16[320,2560]{0,1:T(8,128)(2,1)S(1)}) all-reduce(f32[5]{0:T(128)S(1)} %negate_multiply_fusion, f32[5]{0:T(128)S(1)} %reduce_sum.212, f32[320,2560]{0,1:T(8,128)} %fusion.132), channel_id=1, replica_groups=mesh['seq'=32,'dp'=2,'tensor'=8] {'seq','dp'}, use_global_device_ids=true, to_apply=%region_22.23 | all-reduce | flops 819210 | bytes 4915280 | tf_op jit(solution)/shard_map/psum | solution.py:130
  (294 shorter events, 66.2 us)
Async XLA Ops:
  7.2 6.8 %copy-start.17 = (bf16[1,512,128]{2,1,0:T(8,128)(2,1)S(1)}, bf16[1,512,128]{2,1,0:T(8,128)(2,1)}, u32[]{:S(2)}) copy-start(bf16[1,512,128]{2,1,0:T(8,128)(2,1)} %param.13) | copy-start | bytes 393220
  7.2 8.0 %copy-start.20 = (bf16[1,320,512]{2,1,0:T(8,128)(2,1)S(1)}, bf16[1,320,512]{2,1,0:T(8,128)(2,1)}, u32[]{:S(2)}) copy-start(bf16[1,320,512]{2,1,0:T(8,128)(2,1)} %param.19) | copy-start | bytes 983044
  7.2 50.5 %all-gather.7.cloned.1.call-start = ((), (), s32[]{:S(2)}) async-start(), calls=%async_computation | async-start | bytes 2457600 | tf_op jit(solution)/shard_map/all_gather | solution.py:102
  7.9 142.1 %all-gather.9.cloned.1.call-start = ((), (), s32[]{:S(2)}) async-start(), calls=%async_computation.1 | async-start | bytes 5406720 | tf_op jit(solution)/shard_map/all_gather | solution.py:71
  14.0 19.0 %copy-start.21 = (bf16[1,320,512]{2,1,0:T(8,128)(2,1)S(1)}, bf16[1,320,512]{2,1,0:T(8,128)(2,1)}, u32[]{:S(2)}) copy-start(bf16[1,320,512]{2,1,0:T(8,128)(2,1)} %param.19) | copy-start | bytes 983044
  15.1 204.4 %all-gather.11.cloned.1.call-start = ((), (), s32[]{:S(2)}) async-start(), calls=%async_computation.2 | async-start | bytes 5406720 | tf_op jit(solution)/shard_map/all_gather | solution.py:113
  15.2 11.5 %collective-permute-start = (bf16[320,512]{1,0:T(8,128)(2,1)S(1)}, bf16[320,512]{1,0:T(8,128)(2,1)}, u32[]{:S(2)}, u32[]{:S(2)}) collective-permute-start(bf16[320,512]{1,0:T(8,128)(2,1)S(1)} %bitcast.505), channel_id=1, source_target_pairs={{0,1},{1,2},{2,3},{3,4},{4,5},{5,6},{6,7},{7,0},{8,9},{9,10},{10,1... | collective-permute-start | bytes 983048 | tf_op jit(solution)/shard_map/ppermute | solution.py:91
  18.7 12.2 %collective-permute-start.1 = (bf16[320,512]{1,0:T(8,128)(2,1)S(1)}, bf16[320,512]{1,0:T(8,128)(2,1)}, u32[]{:S(2)}, u32[]{:S(2)}) collective-permute-start(bf16[320,512]{1,0:T(8,128)(2,1)S(1)} %bitcast.506), channel_id=1, source_target_pairs={{0,7},{1,0},{2,1},{3,2},{4,3},{5,4},{6,5},{7,6},{8,15},{9,8},{10,9... | collective-permute-start | bytes 983048 | tf_op jit(solution)/shard_map/ppermute | solution.py:94
  26.6 10.7 %collective-permute-start.2 = (bf16[320,512]{1,0:T(8,128)(2,1)}, bf16[320,512]{1,0:T(8,128)(2,1)S(1)}, u32[]{:S(2)}, u32[]{:S(2)}) collective-permute-start(bf16[320,512]{1,0:T(8,128)(2,1)} %collective-permute-done), channel_id=1, source_target_pairs={{0,1},{1,2},{2,3},{3,4},{4,5},{5,6},{6,7},{7,0},{8,9},{9,10},{10,1... | collective-permute-start | bytes 983048 | tf_op jit(solution)/shard_map/ppermute | solution.py:91
  30.9 13.5 %collective-permute-start.3 = (bf16[320,512]{1,0:T(8,128)(2,1)}, bf16[320,512]{1,0:T(8,128)(2,1)}, u32[]{:S(2)}, u32[]{:S(2)}) collective-permute-start(bf16[320,512]{1,0:T(8,128)(2,1)} %collective-permute-done.1), channel_id=1, source_target_pairs={{0,7},{1,0},{2,1},{3,2},{4,3},{5,4},{6,5},{7,6},{8,15},{9,8},{10,9... | collective-permute-start | bytes 983048 | tf_op jit(solution)/shard_map/ppermute | solution.py:94
  37.3 10.3 %collective-permute-start.4 = (bf16[320,512]{1,0:T(8,128)(2,1)S(1)}, bf16[320,512]{1,0:T(8,128)(2,1)S(1)}, u32[]{:S(2)}, u32[]{:S(2)}) collective-permute-start(bf16[320,512]{1,0:T(8,128)(2,1)S(1)} %collective-permute-done.2), channel_id=1, source_target_pairs={{0,1},{1,2},{2,3},{3,4},{4,5},{5,6},{6,7},{7,0},{8,9},{9,10},{10,1... | collective-permute-start | bytes 983048 | tf_op jit(solution)/shard_map/ppermute | solution.py:91
  44.4 11.3 %collective-permute-start.5 = (bf16[320,512]{1,0:T(8,128)(2,1)}, bf16[320,512]{1,0:T(8,128)(2,1)S(1)}, u32[]{:S(2)}, u32[]{:S(2)}) collective-permute-start(bf16[320,512]{1,0:T(8,128)(2,1)} %collective-permute-done.3), channel_id=1, source_target_pairs={{0,7},{1,0},{2,1},{3,2},{4,3},{5,4},{6,5},{7,6},{8,15},{9,8},{10,9... | collective-permute-start | bytes 983048 | tf_op jit(solution)/shard_map/ppermute | solution.py:94
  47.6 10.1 %collective-permute-start.6 = (bf16[320,512]{1,0:T(8,128)(2,1)S(1)}, bf16[320,512]{1,0:T(8,128)(2,1)S(1)}, u32[]{:S(2)}, u32[]{:S(2)}) collective-permute-start(bf16[320,512]{1,0:T(8,128)(2,1)S(1)} %collective-permute-done.4), channel_id=1, source_target_pairs={{0,1},{1,2},{2,3},{3,4},{4,5},{5,6},{6,7},{7,0},{8,9},{9,10},{10,1... | collective-permute-start | bytes 983048 | tf_op jit(solution)/shard_map/ppermute | solution.py:91
  57.7 5.0 copy-start.3
  61.2 85.8 %copy-start.22 = (f32[1,5,512]{2,0,1:T(1,128)S(1)}, f32[1,5,512]{2,0,1:T(1,128)}, u32[]{:S(2)}) copy-start(f32[1,5,512]{2,0,1:T(1,128)} %param.15) | copy-start | bytes 30724
  61.2 86.0 %copy-start.19 = (bf16[1,512,128]{2,1,0:T(8,128)(2,1)S(1)}, bf16[1,512,128]{2,1,0:T(8,128)(2,1)}, u32[]{:S(2)}) copy-start(bf16[1,512,128]{2,1,0:T(8,128)(2,1)} %param.14) | copy-start | bytes 393220
  61.3 86.0 %copy-start.27 = (f32[5]{0:T(128)S(1)}, f32[5]{0:T(128)}, u32[]{:S(2)}) copy-start(f32[5]{0:T(128)} %param.17) | copy-start | bytes 64
  62.6 86.9 %copy-start.8 = (bf16[320,512]{1,0:T(8,128)(2,1)S(1)}, bf16[320,512]{1,0:T(8,128)(2,1)}, u32[]{:S(2)}) copy-start(bf16[320,512]{1,0:T(8,128)(2,1)} %copy-done.7) | copy-start | bytes 983044
  150.0 10.6 %copy-start.24 = (f32[2,5,1,256]{3,1,2,0:T(8,128)S(1)}, f32[2,5,1,256]{3,1,2,0:T(8,128)}, u32[]{:S(2)}) copy-start(f32[2,5,1,256]{3,1,2,0:T(8,128)} %custom-call.9) | copy-start | bytes 30724
  150.0 10.6 %copy-start.25 = (f32[2,5,1,256]{3,1,2,0:T(8,128)S(1)}, f32[2,5,1,256]{3,1,2,0:T(8,128)}, u32[]{:S(2)}) copy-start(f32[2,5,1,256]{3,1,2,0:T(8,128)} %custom-call.12) | copy-start | bytes 30724
  150.0 10.6 %copy-start.28 = (f32[2,5]{1,0:T(2,128)S(1)}, f32[2,5]{1,0:T(2,128)}, u32[]{:S(2)}) copy-start(f32[2,5]{1,0:T(2,128)} %custom-call.10) | copy-start | bytes 124
  150.0 10.5 %copy-start.30 = (f32[2,5,1,1]{1,3,2,0:T(1,128)S(1)}, f32[2,5,1,1]{1,3,2,0:T(1,128)}, u32[]{:S(2)}) copy-start(f32[2,5,1,1]{1,3,2,0:T(1,128)} %custom-call.11) | copy-start | bytes 124
  164.6 4.1 copy-start
  168.6 4.8 copy-start.5
  178.3 4.1 copy-start
  182.4 4.8 copy-start.5
  191.1 5.5 copy-start.10
  243.3 5.4 copy-start.11
  243.3 6.8 %copy-start.14 = (f32[2,256,128]{2,1,0:T(8,128)S(1)}, f32[2,256,128]{2,1,0:T(8,128)}, u32[]{:S(2)}) copy-start(f32[2,256,128]{2,1,0:T(8,128)} %get-tuple-element.2148) | copy-start | bytes 786436 | tf_op jit(solution)/shard_map/transpose(jvp())/while
  265.8 5.4 copy-start.11
  265.9 6.8 %copy-start.14 = (f32[2,256,128]{2,1,0:T(8,128)S(1)}, f32[2,256,128]{2,1,0:T(8,128)}, u32[]{:S(2)}) copy-start(f32[2,256,128]{2,1,0:T(8,128)} %get-tuple-element.2148) | copy-start | bytes 786436 | tf_op jit(solution)/shard_map/transpose(jvp())/while
  274.8 38.8 %copy-start.23 = (f32[1,5,512]{2,0,1:T(1,128)S(1)}, f32[1,5,512]{2,0,1:T(1,128)}, u32[]{:S(2)}) copy-start(f32[1,5,512]{2,0,1:T(1,128)} %param.15) | copy-start | bytes 30724
  (18 other events, 40.5 us)
Sparse Core Ops, SparseCore 0:
  10.1 22.4 all-gather.6
  36.4 92.3 all-gather.8
  131.9 87.5 all-gather.10
